TPU v7x, 128 devices: a whole 4x4x4 slice. The times are simulated.
128 devices in a mesh: roll: 16 (over z, y_hi, core), kvh: 8 (over y_lo, x).
Axes of the slice: x: 4, y: 4 (y_hi: 2, y_lo: 2; y = y_hi * 2 + y_lo), z: 4, core: 2. Of those that a mesh axis runs over, the one named last changes fastest.
Arguments:
- out_grad: bfloat16 [16, 256, 5120], P('roll', 'kvh'), may hold values from -48 to 48
- out_weight: bfloat16 [8, 5, 128, 5120], P('kvh'), may hold values from -0.078125 to 0.078125
- queries: bfloat16 [16, 256, 8, 5, 128], P('roll', None, 'kvh'), may hold values from -16 to 16
- keys_new: bfloat16 [16, 256, 8, 128], P('roll', None, 'kvh'), may hold values from -16 to 16
- values_new: bfloat16 [16, 256, 8, 128], P('roll', None, 'kvh'), may hold values from -6 to 6
- keys_prompt: bfloat16 [4096, 8, 128], P('roll', 'kvh'), may hold values from -6 to 6
- values_prompt: bfloat16 [4096, 8, 128], P('roll', 'kvh'), may hold values from -6 to 6
- offsets: int32 [16], P('roll'), may hold values from 0 to 3840
Outputs:
- grad_queries: bfloat16 [16, 256, 8, 5, 128], P('roll', None, 'kvh')
- grad_keys_new: bfloat16 [16, 256, 8, 128], P('roll', None, 'kvh')
- grad_values_new: bfloat16 [16, 256, 8, 128], P('roll', None, 'kvh')
- grad_keys_prompt: bfloat16 [4096, 8, 128], P('roll', 'kvh')
- grad_values_prompt: bfloat16 [4096, 8, 128], P('roll', 'kvh')
Inputs may be any that keep to these rules, and one draw needn't show every extreme that they name: `offsets`: each slice lies inside a response of 4096 tokens.
All inputs are finite; a program needn't handle non-finite values.
Results may differ from a plain program's by a relative error of at most 0.015.
The roundings to bfloat16 on the way count: a program that leaves them out, or rounds other values in their place, can miss the bound.
Values may be sent and summed in bfloat16 or wider, within the bound.
A program may use at most 64 MiB of HBM per device.

v0:
```python
import math
import jax
import jax.numpy as jnp
from jax import lax
from jax.sharding import PartitionSpec as P

theta_base = 1000000.0


def rotation(positions, head_width):
    half_width = head_width // 2
    frequency = jnp.power(theta_base, -(jnp.arange(half_width, dtype=jnp.float32) / half_width))
    angles = positions.astype(jnp.float32)[:, None] * frequency[None, :]
    return (jnp.cos(angles), jnp.sin(angles))


def rotate(vectors, cos_part, sin_part, direction):
    half_width = vectors.shape[-1] // 2
    front_half = vectors[..., :half_width]
    back_half = vectors[..., half_width:]
    return jnp.concatenate(
        [
            front_half * cos_part - direction * back_half * sin_part,
            back_half * cos_part + direction * front_half * sin_part,
        ],
        axis=-1,
    )


def inner_dot(left, right):
    return lax.dot_general(
        left, right, (((1,), (1,)), ((), ())), preferred_element_type=jnp.float32
    )


def outer_sum(left, right):
    return lax.dot_general(
        left, right, (((0,), (0,)), ((), ())), preferred_element_type=jnp.float32
    )


def block_grads(context, key_block, value_block):
    query_rows, grad_rows, log_total, row_delta, score_scale = context
    scores = inner_dot(query_rows, key_block) * score_scale
    attn_probs = jnp.exp(scores - log_total[:, None]).astype(jnp.bfloat16)
    prob_grad = inner_dot(grad_rows, value_block)
    score_grad = (
        attn_probs.astype(jnp.float32) * (prob_grad - row_delta[:, None]) * score_scale
    ).astype(jnp.bfloat16)
    return (attn_probs, score_grad)


def local(out_grad, out_weight, queries, keys_new, values_new, keys_prompt, values_prompt, offsets):
    roll_local, seq_len, kv_local, group_size, head_width = queries.shape
    prompt_local = keys_prompt.shape[0]
    prompt_total = prompt_local * lax.axis_size("roll")
    score_scale = head_width ** (-0.5)
    row_total = roll_local * seq_len * group_size
    attn_grad = jnp.einsum(
        "rsc,ghdc->rsghd",
        lax.all_gather(out_grad, "kvh", axis=1, tiled=True),
        out_weight,
        preferred_element_type=jnp.float32,
    ).astype(jnp.bfloat16)
    cached_keys, cached_values = (
        lax.all_gather(keys_prompt, "roll", axis=0, tiled=True),
        lax.all_gather(values_prompt, "roll", axis=0, tiled=True),
    )
    positions = prompt_total + offsets[:, None] + jnp.arange(seq_len, dtype=jnp.int32)[None, :]
    cos_flat, sin_flat = rotation(positions.reshape(-1), head_width)
    cos_four = cos_flat.reshape(roll_local, seq_len, 1, head_width // 2)
    sin_four = sin_flat.reshape(roll_local, seq_len, 1, head_width // 2)
    query_rot = rotate(
        queries.astype(jnp.float32), cos_four[:, :, :, None], sin_four[:, :, :, None], 1.0
    ).astype(jnp.bfloat16)
    key_rot = rotate(keys_new.astype(jnp.float32), cos_four, sin_four, 1.0).astype(jnp.bfloat16)
    block_len = math.gcd(prompt_total, 512)
    block_count = prompt_total // block_len
    causal = (jnp.arange(seq_len)[None, :] <= jnp.arange(seq_len)[:, None])[None, :, None, :]
    contexts = []
    query_head = query_rot[:, :, 0]
    key_head = key_rot[:, :, 0]
    value_head = values_new[:, :, 0]
    grad_head = attn_grad[:, :, 0]
    query_rows = query_head.reshape(row_total, head_width)
    grad_rows = grad_head.reshape(row_total, head_width)
    key_blocks = cached_keys[:, 0].reshape(block_count, block_len, head_width)
    value_blocks = cached_values[:, 0].reshape(block_count, block_len, head_width)
    near_scores = (
        jnp.einsum("rshd,rtd->rsht", query_head, key_head, preferred_element_type=jnp.float32)
        * score_scale
    )
    near_scores = jnp.where(causal, near_scores, -jnp.inf)
    near_max = jnp.max(near_scores, axis=3, keepdims=True)
    near_sum = jnp.sum(jnp.exp(near_scores - near_max), axis=3)

    def stat_step(running, key_block):
        old_max, old_sum = running
        scores = inner_dot(query_rows, key_block) * score_scale
        new_max = jnp.maximum(old_max, jnp.max(scores, axis=1))
        new_sum = old_sum * jnp.exp(old_max - new_max) + jnp.sum(
            jnp.exp(scores - new_max[:, None]), axis=1
        )
        return ((new_max, new_sum), None)

    stats, unused = lax.scan(
        stat_step, (near_max.reshape(row_total), near_sum.reshape(row_total)), key_blocks
    )
    log_total = stats[0] + jnp.log(stats[1])
    log_shaped = log_total.reshape(roll_local, seq_len, group_size, 1)
    near_probs = jnp.where(causal, jnp.exp(near_scores - log_shaped), 0.0).astype(jnp.bfloat16)
    near_output = jnp.einsum(
        "rsht,rtd->rshd", near_probs, value_head, preferred_element_type=jnp.float32
    ).reshape(row_total, head_width)

    def output_step(total_out, blocks):
        scores = inner_dot(query_rows, blocks[0]) * score_scale
        attn_probs = jnp.exp(scores - log_total[:, None]).astype(jnp.bfloat16)
        return (
            total_out + jnp.dot(attn_probs, blocks[1], preferred_element_type=jnp.float32),
            None,
        )

    output, unused = lax.scan(output_step, near_output, (key_blocks, value_blocks))
    row_delta = jnp.sum(grad_rows.astype(jnp.float32) * output, axis=1)
    context = (query_rows, grad_rows, log_total, row_delta, score_scale)
    contexts.append(context)
    near_prob_grad = jnp.einsum(
        "rshd,rtd->rsht", grad_head, value_head, preferred_element_type=jnp.float32
    )
    delta_shaped = row_delta.reshape(roll_local, seq_len, group_size, 1)
    near_grad = (
        near_probs.astype(jnp.float32) * (near_prob_grad - delta_shaped) * score_scale
    ).astype(jnp.bfloat16)
    near_query = jnp.einsum(
        "rsht,rtd->rshd", near_grad, key_head, preferred_element_type=jnp.float32
    )
    key_new_grad = jnp.einsum(
        "rsht,rshd->rtd", near_grad, query_head, preferred_element_type=jnp.float32
    )
    value_new_grad = jnp.einsum(
        "rsht,rshd->rtd", near_probs, grad_head, preferred_element_type=jnp.float32
    )
    zero_rows = jnp.zeros((row_total, head_width), jnp.float32)

    def grad_step(total_grad, blocks):
        attn_probs, score_grad = block_grads(context, blocks[0], blocks[1])
        block_term = jnp.stack(
            [outer_sum(score_grad, query_rows), outer_sum(attn_probs, grad_rows)], axis=1
        )
        return (
            total_grad + jnp.dot(score_grad, blocks[0], preferred_element_type=jnp.float32),
            block_term,
        )

    far_query, block_terms = lax.scan(grad_step, zero_rows, (key_blocks, value_blocks))
    term_list = [block_terms.reshape(prompt_total, 2, head_width)]
    query_grad = far_query.reshape(roll_local, seq_len, group_size, head_width) + near_query
    query_list = [rotate(query_grad, cos_four, sin_four, -1.0).astype(jnp.bfloat16)]
    key_list = [
        rotate(key_new_grad, cos_four[:, :, 0], sin_four[:, :, 0], -1.0).astype(jnp.bfloat16)
    ]
    value_list = [value_new_grad.astype(jnp.bfloat16)]
    reduced = lax.psum_scatter(
        jnp.stack(term_list, axis=1).astype(jnp.bfloat16), "roll", scatter_dimension=0, tiled=True
    ).astype(jnp.float32)
    grad_queries = jnp.stack(query_list, axis=2)
    grad_keys_new = jnp.stack(key_list, axis=2)
    grad_values_new = jnp.stack(value_list, axis=2)
    return (
        grad_queries,
        grad_keys_new,
        grad_values_new,
        reduced[:, :, 0].astype(jnp.bfloat16),
        reduced[:, :, 1].astype(jnp.bfloat16),
    )


def solution(mesh):
    placed = (
        P("roll", "kvh", None),
        P("kvh", None, None, None),
        P("roll", None, "kvh", None, None),
        P("roll", None, "kvh", None),
        P("roll", None, "kvh", None),
        P("roll", "kvh", None),
        P("roll", "kvh", None),
        P("roll"),
    )
    return jax.shard_map(
        local,
        mesh=mesh,
        in_specs=placed,
        out_specs=(
            P("roll", None, "kvh", None, None),
            P("roll", None, "kvh", None),
            P("roll", None, "kvh", None),
            P("roll", "kvh", None),
            P("roll", "kvh", None),
        ),
        check_vma=False,
    )
```

profile of v0, /device:TPU:0, one launch (start us, length us, event | category | flops | bytes accessed | tf_op | source)
XLA Modules:
  0.0 288.3 jit_solution(14173419729338895202)
XLA Ops:
  10.2 0.9 convert_element_type.126
  11.0 0.9 broadcast_multiply_fusion
  12.0 1.2 fusion.70
  13.4 1.0 convert_element_type.124
  15.0 0.9 concatenate.68
  16.2 0.9 concatenate.69
  19.1 38.9 %all-gather.4.cloned.1.call-done = bf16[4096,1,128]{2,0,1:T(8,128)(2,1)} async-done(((bf16[256,1,128]{2,0,1:T(8,128)(2,1)}), bf16[4096,1,128]{2,0,1:T(8,128)(2,1)}) %all-gather.4.cloned.1.call-update) | async-done | bytes 1048592 | tf_op jit(solution)/shard_map/all_gather | solution.py:66
  58.0 15.1 %while.35 = (s32[]{:T(128)}, f32[1280]{0:T(1024)S(1)}, f32[1280]{0:T(1024)S(1)}, bf16[8,512,128]{2,1,0:T(8,128)(2,1)}, bf16[1280,128]{1,0:T(8,128)(2,1)S(1)}, /*index=5*/s32[]{:T(128)}) while((s32[]{:T(128)}, f32[1280]{0:T(1024)S(1)}, f32[1280]{0:T(1024)S(1)}, bf16[8,512,128]{2,1,0:T(8,128)(2,1)}, bf16[1280,128]{1,0:T(8,128)(2,1)S(1)}, ...), condition=%wide.region_5.6_spmd, body=%wide.region_2.5_spmd.sunk | while | flops 170396160 | bytes 5768273 | solution.py:106
  58.0 1.4 fusion.112
  59.9 1.4 fusion.112
  61.7 1.4 fusion.112
  63.6 1.4 fusion.112
  65.5 1.4 fusion.112
  67.4 1.4 fusion.112
  69.3 1.4 fusion.112
  71.2 1.4 fusion.112
  74.0 1.1 dot_general.51
  75.1 1.4 fusion.67
  76.6 27.6 %all-gather.6.cloned.1.call-done = bf16[4096,1,128]{2,0,1:T(8,128)(2,1)} async-done(((bf16[256,1,128]{2,0,1:T(8,128)(2,1)}), bf16[4096,1,128]{2,0,1:T(8,128)(2,1)}) %all-gather.6.cloned.1.call-update) | async-done | bytes 1048592 | tf_op jit(solution)/shard_map/all_gather | solution.py:67
  104.1 15.5 %while.36 = (s32[]{:T(128)}, f32[1280,128]{1,0:T(8,128)S(1)}, bf16[8,512,128]{2,1,0:T(8,128)(2,1)}, bf16[1280,128]{1,0:T(8,128)(2,1)S(1)}, f32[1280]{0:T(1024)S(1)}, /*index=5*/bf16[8,512,128]{2,1,0:T(8,128)(2,1)}, s32[]{:T(128)}) while((s32[]{:T(128)}, f32[1280,128]{1,0:T(8,128)S(1)}, bf16[8,512,128]{2,1,0:T(8,128)(2,1)}, ...), condition=%wide.region_7.8_spmd, body=%wide.region_6.7_spmd.sunk | while | flops 337674240 | bytes 1906773 | solution.py:124
  104.1 1.9 convolution_add_fusion.5
  106.0 1.9 convolution_add_fusion.5
  108.0 1.9 convolution_add_fusion.5
  109.9 1.9 convolution_add_fusion.5
  111.9 1.9 convolution_add_fusion.5
  113.8 1.9 convolution_add_fusion.5
  115.7 1.9 convolution_add_fusion.5
  117.7 1.9 convolution_add_fusion.5
  119.6 27.1 %all-gather.8.cloned.1.call-done = bf16[1,256,5120]{2,1,0:T(8,128)(2,1)} async-done(((bf16[1,32,5120]{2,1,0:T(8,128)(2,1)}), bf16[1,256,5120]{2,1,0:T(8,128)(2,1)}) %all-gather.8.cloned.1.call-update) | async-done | bytes 2621456 | tf_op jit(solution)/shard_map/all_gather | solution.py:61
  146.7 5.9 %fusion.41 = bf16[256,5,128]{2,0,1:T(8,128)(2,1)S(1)} fusion(bf16[1,5,128,5120]{3,2,1,0:T(8,128)(2,1)} %param.15, bf16[1,256,5120]{2,1,0:T(8,128)(2,1)} %all-gather.8.cloned.1.call-done), kind=kOutput, calls=%fused_computation.54 | convolution fusion | flops 1677885440 | bytes 9502720 | tf_op jit(solution)/shard_map/rsc,ghdc->rsghd/dot_general | solution.py:59
  152.6 1.0 copy.60
  153.6 1.2 reshape_squeeze.12
  155.1 51.2 %while.37 = (s32[]{:T(128)}, f32[1280,128]{1,0:T(8,128)S(1)}, bf16[8,512,2,128]{3,1,2,0:T(8,128)(2,1)}, bf16[8,512,128]{2,1,0:T(8,128)(2,1)}, bf16[1280,128]{1,0...) while((s32[]{:T(128)}, f32[1280,128]{1,0:T(8,128)S(1)}, ...), condition=%wide.region_10.11_spmd.clone, body=%wide.region_9.10_spmd.clone.sunk | while | flops 844955648 | bytes 11675791 | solution.py:156
  155.1 1.5 fusion.126
  157.1 1.5 fusion.127
  159.1 1.7 convolution_add_fusion.6
  161.5 1.5 fusion.126
  163.5 1.5 fusion.127
  165.5 1.7 convolution_add_fusion.6
  167.9 1.5 fusion.126
  169.9 1.5 fusion.127
  171.9 1.7 convolution_add_fusion.6
  174.3 1.5 fusion.126
  176.3 1.5 fusion.127
  178.3 1.7 convolution_add_fusion.6
  180.7 1.5 fusion.126
  182.7 1.5 fusion.127
  184.7 1.7 convolution_add_fusion.6
  187.1 1.5 fusion.126
  189.1 1.5 fusion.127
  191.1 1.7 convolution_add_fusion.6
  193.5 1.5 fusion.126
  195.5 1.5 fusion.127
  197.5 1.7 convolution_add_fusion.6
  199.9 1.5 fusion.126
  201.9 1.5 fusion.127
  203.9 1.7 convolution_add_fusion.6
  206.3 3.1 %copy.68 = bf16[8,512,2,128]{3,1,0,2:T(8,128)(2,1)} copy(bf16[8,512,2,128]{3,1,2,0:T(8,128)(2,1)} %get-tuple-element.117) | data formatting | bytes 4194304 | tf_op jit(solution)/shard_map/convert_element_type | solution.py:165
  212.2 1.1 copy.65
  213.3 1.6 fusion.40
  215.0 0.9 copy.69
  215.9 1.0 fusion.47
  216.9 63.3 %reduce-scatter.2.cloned.1.call-done = bf16[256,1,2,128]{3,0,2,1:T(8,128)(2,1)} async-done(((bf16[4096,1,2,128]{3,0,2,1:T(8,128)(2,1)}), bf16[256,1,2,128]{3,0,2,1:T(8,128)(2,1)}) %reduce-scatter.2.cloned.1.call-update) | async-done | bytes 131088 | tf_op jit(solution)/shard_map/reduce_scatter | solution.py:164
  280.3 1.5 slice_bitcast_fusion
  (121 shorter events, 26.5 us)
Async XLA Ops:
  7.2 68.0 %copy-start = (bf16[1,256,1,128]{3,1,2,0:T(8,128)(2,1)S(1)}, bf16[1,256,1,128]{3,1,2,0:T(8,128)(2,1)}, u32[]{:S(2)}) copy-start(bf16[1,256,1,128]{3,1,2,0:T(8,128)(2,1)} %param.18) | copy-start | bytes 196612
  7.2 50.8 %all-gather.4.cloned.1.call-start = ((), (), s32[]{:S(2)}) async-start(), calls=%async_computation.1 | async-start | bytes 1114112 | tf_op jit(solution)/shard_map/all_gather | solution.py:66
  7.9 96.2 %all-gather.6.cloned.1.call-start = ((), (), s32[]{:S(2)}) async-start(), calls=%async_computation.2 | async-start | bytes 1114112 | tf_op jit(solution)/shard_map/all_gather | solution.py:67
  8.7 138.0 %all-gather.8.cloned.1.call-start = ((), (), s32[]{:S(2)}) async-start(), calls=%async_computation.3 | async-start | bytes 2949120 | tf_op jit(solution)/shard_map/all_gather | solution.py:61
  9.4 270.9 %reduce-scatter.2.cloned.1.call-start = ((), (), s32[]{:S(2)}) async-start(), calls=%async_computation.4 | async-start | bytes 2228224 | tf_op jit(solution)/shard_map/reduce_scatter | solution.py:164
  14.7 3.0 %copy-start.1 = (bf16[1,256,1,5,64]{4,1,3,2,0:T(8,128)(2,1)}, bf16[1,256,1,5,64]{4,1,3,2,0:T(8,128)(2,1)S(1)}, u32[]{:S(2)}) copy-start(bf16[1,256,1,5,64]{4,1,3,2,0:T(8,128)(2,1)S(1)} %get-tuple-element.210) | copy-start | bytes 491524
  14.7 3.0 %copy-start.3 = (bf16[1,256,1,5,64]{4,1,3,2,0:T(8,128)(2,1)}, bf16[1,256,1,5,64]{4,1,3,2,0:T(8,128)(2,1)S(1)}, u32[]{:S(2)}) copy-start(bf16[1,256,1,5,64]{4,1,3,2,0:T(8,128)(2,1)S(1)} %get-tuple-element.211) | copy-start | bytes 491524
  14.7 2.4 copy-start.9
  17.1 1.8 copy-start.7
  17.7 1.2 copy-start.8
  152.6 57.2 %copy-start.5 = (bf16[256,5,128]{2,0,1:T(8,128)(2,1)}, bf16[256,5,128]{2,0,1:T(8,128)(2,1)S(1)}, u32[]{:S(2)}) copy-start(bf16[256,5,128]{2,0,1:T(8,128)(2,1)S(1)} %fusion.41) | copy-start | bytes 983044
  209.4 1.0 copy-start.2
  209.4 1.1 copy-start.4
  211.0 2.3 copy-start.10
  212.2 2.7 copy-start.11
  213.3 2.6 copy-start.6
Sparse Core Ops, SparseCore 0:
  10.5 47.4 all-gather.3
  60.4 43.6 all-gather.5
  105.8 40.8 all-gather.7
  209.6 70.6 reduce-scatter.1
where the time goes:
time: 289 us; the launch traced here: 288 us
  waiting for transfers between devices  159 us (55%)
  matrix products  83.2 us (29%)
  local copies, waits for them, and re-layouts  15.5 us (5%)
  other arithmetic  15.2 us (5%)
  between operations  14.7 us (5%)
    reduce_scatter x1, waiting for transfers between devices, local(): lax.psum_scatter(jnp.stack(term_list, axis=1).astype(jnp.bfloat16), 'roll...  63.3 us
    all_gather x1, waiting for transfers between devices, local(): lax.all_gather(keys_prompt, 'roll', axis=0, tiled=True)  38.9 us
    dot_general x24, matrix products, inner_dot(): lax.dot_general(left, right, (((1,), (1,)), ((), ())), preferred_element_...  35 us
    all_gather x1, waiting for transfers between devices, local(): lax.all_gather(values_prompt, 'roll', axis=0, tiled=True)  27.6 us
    all_gather x1, waiting for transfers between devices, local(): lax.all_gather(out_grad, 'kvh', axis=1, tiled=True)  27.1 us
    dot_general x8, matrix products, output_step(): jnp.dot(attn_probs, blocks[1], preferred_element_type=jnp.float32)  15.3 us
    dot_general x8, matrix products, grad_step(): jnp.dot(score_grad, blocks[0], preferred_element_type=jnp.float32)  13.5 us
    dot_general x16, matrix products, outer_sum(): lax.dot_general(left, right, (((0,), (0,)), ((), ())), preferred_element_...  8.1 us
  transfers between devices with their start and end apart: 4, of which 4 were waited for; matrix products, arithmetic and copies ran while one was open for 17% of the time, Pallas kernels for 0%

commit v1 on v0

--- a/solution.py
+++ b/solution.py
@@ -58,7 +58,9 @@
     row_total = roll_local * seq_len * group_size
     attn_grad = jnp.einsum(
         "rsc,ghdc->rsghd",
-        lax.all_gather(out_grad, "kvh", axis=1, tiled=True),
+        jnp.concatenate(
+            lax.all_to_all(jnp.stack([out_grad] * lax.axis_size("kvh")), "kvh", 0, 0), axis=1
+        ),
         out_weight,
         preferred_element_type=jnp.float32,
     ).astype(jnp.bfloat16)

time: 289 us -> 277 us (0.958)
  waiting for transfers between devices: 159 us -> 140 us
  starting transfers between devices: 0.15 us -> 5.64 us
  local copies, waits for them, and re-layouts: 15.5 us -> 19.7 us
    all_gather x1 -> x0, waiting for transfers between devices: 27.1 us -> none  [local(): lax.all_gather(out_grad, 'kvh', axis=1, tiled=True)]
    all_gather x1, waiting for transfers between devices: 38.9 us -> 47.3 us  [local(): lax.all_gather(keys_prompt, 'roll', axis=0, tiled=True)]
    all_to_all x0 -> x1, starting transfers between devices: none -> 5.53 us  [local(): lax.all_to_all(jnp.stack([out_grad] * lax.axis_size('kvh')), 'kvh', 0, 0)]
    another operation x2 -> x3, local copies, waits for them, and re-layouts: 0.48 us -> 4.07 us  [the longest x1 2.8 us: local(): jnp.stack([out_grad] * lax.axis_size('kvh'))]
  transfers between devices with their start and end apart: 4 -> 4, of which waited for: 4 -> 3; matrix products, arithmetic and copies ran while one was open for 17% -> 18% of each run, Pallas kernels for 0% -> 0%
where the time goes in v1:
time: 277 us; the launch traced here: 276 us
  waiting for transfers between devices  140 us (51%)
  matrix products  82 us (30%)
  local copies, waits for them, and re-layouts  19.7 us (7%)
  between operations  14.8 us (5%)
  other arithmetic  12.7 us (5%)
  starting transfers between devices  5.64 us (2%)
    reduce_scatter x1, waiting for transfers between devices, local(): lax.psum_scatter(jnp.stack(term_list, axis=1).astype(jnp.bfloat16), 'roll...  64 us
    all_gather x1, waiting for transfers between devices, local(): lax.all_gather(keys_prompt, 'roll', axis=0, tiled=True)  47.3 us
    dot_general x24, matrix products, inner_dot(): lax.dot_general(left, right, (((1,), (1,)), ((), ())), preferred_element_...  35 us
    all_gather x1, waiting for transfers between devices, local(): lax.all_gather(values_prompt, 'roll', axis=0, tiled=True)  27.6 us
    dot_general x8, matrix products, output_step(): jnp.dot(attn_probs, blocks[1], preferred_element_type=jnp.float32)  15.3 us
    dot_general x8, matrix products, grad_step(): jnp.dot(score_grad, blocks[0], preferred_element_type=jnp.float32)  13.4 us
    dot_general x16, matrix products, outer_sum(): lax.dot_general(left, right, (((0,), (0,)), ((), ())), preferred_element_...  8.11 us
    dot_general x1, matrix products, local(): jnp.einsum('rsc,ghdc->rsghd', jnp.concatenate(lax.all_to_all(jnp.stack([o...  5.89 us
  transfers between devices with their start and end apart: 4, of which 3 were waited for; matrix products, arithmetic and copies ran while one was open for 18% of the time, Pallas kernels for 0%

profile of v1, /device:TPU:0, one launch (start us, length us, event | category | flops | bytes accessed | tf_op | source)
XLA Modules:
  0.0 276.0 jit_solution(3768227934715048195)
XLA Ops:
  7.9 2.8 %stack.10 = bf16[8,1,32,5120]{3,2,1,0:T(8,128)(2,1)} broadcast(bf16[32,5120]{1,0:T(8,128)(2,1)} %bitcast.149), dimensions={2,3} | broadcast | bytes 2949120 | tf_op jit(solution)/shard_map/stack | solution.py:62
  10.7 5.5 %all-to-all-start = ((bf16[8,1,32,5120]{3,2,1,0:T(8,128)(2,1)}), bf16[8,1,32,5120]{3,2,1,0:T(8,128)(2,1)}, u32[]{:S(2)}, u32[]{:S(2)}) async-start(bf16[8,1,32,5120]{3,2,1,0:T(8,128)(2,1)} %stack.10), calls=%async_computation | async-start | bytes 5242880 | tf_op jit(solution)/shard_map/all_to_all | solution.py:62
  17.8 0.9 broadcast_multiply_fusion
  20.2 1.0 copy.57
  21.8 0.8 copy.58
  23.4 1.1 reshape_broadcast_in_dim.3
  24.8 1.2 concatenate.69
  26.2 47.3 %all-gather.3.cloned.1.call-done = bf16[4096,1,128]{2,0,1:T(8,128)(2,1)} async-done(((bf16[256,1,128]{2,0,1:T(8,128)(2,1)}), bf16[4096,1,128]{2,0,1:T(8,128)(2,1)}) %all-gather.3.cloned.1.call-update) | async-done | bytes 1048592 | tf_op jit(solution)/shard_map/all_gather | solution.py:68
  73.5 15.1 %while.35 = (s32[]{:T(128)}, f32[1280]{0:T(1024)S(1)}, f32[1280]{0:T(1024)S(1)}, bf16[8,512,128]{2,1,0:T(8,128)(2,1)}, bf16[1280,128]{1,0:T(8,128)(2,1)S(1)}, /*index=5*/s32[]{:T(128)}) while((s32[]{:T(128)}, f32[1280]{0:T(1024)S(1)}, f32[1280]{0:T(1024)S(1)}, bf16[8,512,128]{2,1,0:T(8,128)(2,1)}, bf16[1280,128]{1,0:T(8,128)(2,1)S(1)}, ...), condition=%wide.region_5.6_spmd, body=%wide.region_2.5_spmd.sunk | while | flops 170396160 | bytes 5768773 | solution.py:108
  73.5 1.4 fusion.110
  75.4 1.4 fusion.110
  77.3 1.4 fusion.110
  79.2 1.4 fusion.110
  81.1 1.4 fusion.110
  82.9 1.4 fusion.110
  84.8 1.4 fusion.110
  86.7 1.4 fusion.110
  89.6 1.1 dot_general.51
  90.7 1.4 fusion.64
  92.1 27.6 %all-gather.5.cloned.1.call-done = bf16[4096,1,128]{2,0,1:T(8,128)(2,1)} async-done(((bf16[256,1,128]{2,0,1:T(8,128)(2,1)}), bf16[4096,1,128]{2,0,1:T(8,128)(2,1)}) %all-gather.5.cloned.1.call-update) | async-done | bytes 1048592 | tf_op jit(solution)/shard_map/all_gather | solution.py:69
  119.7 15.5 %while.36 = (s32[]{:T(128)}, f32[1280,128]{1,0:T(8,128)S(1)}, bf16[8,512,128]{2,1,0:T(8,128)(2,1)}, bf16[1280,128]{1,0:T(8,128)(2,1)S(1)}, f32[1280]{0:T(1024)S(1)}, /*index=5*/bf16[8,512,128]{2,1,0:T(8,128)(2,1)}, s32[]{:T(128)}) while((s32[]{:T(128)}, f32[1280,128]{1,0:T(8,128)S(1)}, bf16[8,512,128]{2,1,0:T(8,128)(2,1)}, ...), condition=%wide.region_7.8_spmd, body=%wide.region_6.7_spmd.sunk | while | flops 337674240 | bytes 1906765 | solution.py:126
  119.7 1.9 convolution_add_fusion.5
  121.6 1.9 convolution_add_fusion.5
  123.5 1.9 convolution_add_fusion.5
  125.5 1.9 convolution_add_fusion.5
  127.4 1.9 convolution_add_fusion.5
  129.4 1.9 convolution_add_fusion.5
  131.3 1.9 convolution_add_fusion.5
  133.2 1.9 convolution_add_fusion.5
  135.2 5.9 %fusion.40 = bf16[256,5,128]{2,0,1:T(8,128)(2,1)S(1)} fusion(bf16[256,5120,1]{1,0,2:T(8,128)(2,1)} %bitcast.13, bf16[1,5,128,5120]{3,2,1,0:T(8,128)(2,1)} %param.15), kind=kOutput, calls=%fused_computation.53 | convolution fusion | flops 1677885440 | bytes 9502720 | tf_op jit(solution)/shard_map/rsc,ghdc->rsghd/dot_general | solution.py:59
  141.1 1.0 copy.60
  142.1 1.2 reshape_squeeze.12
  143.6 51.3 %while.37 = (s32[]{:T(128)}, f32[1280,128]{1,0:T(8,128)S(1)}, bf16[8,512,2,128]{3,1,2,0:T(8,128)(2,1)}, bf16[8,512,128]{2,1,0:T(8,128)(2,1)}, bf16[1280,128]{1,0...) while((s32[]{:T(128)}, f32[1280,128]{1,0:T(8,128)S(1)}, ...), condition=%wide.region_10.11_spmd.clone, body=%wide.region_9.10_spmd.clone.sunk | while | flops 844955648 | bytes 11677815 | solution.py:158
  143.6 1.5 fusion.124
  145.1 1.5 fusion.125
  148.3 1.7 convolution_add_fusion.6
  150.0 1.5 fusion.124
  151.5 1.5 fusion.125
  154.7 1.7 convolution_add_fusion.6
  156.4 1.5 fusion.124
  157.9 1.5 fusion.125
  161.1 1.7 convolution_add_fusion.6
  162.8 1.5 fusion.124
  164.3 1.5 fusion.125
  167.5 1.7 convolution_add_fusion.6
  169.2 1.5 fusion.124
  170.7 1.5 fusion.125
  173.2 0.7 fusion.126
  173.9 1.7 convolution_add_fusion.6
  175.6 1.5 fusion.124
  177.1 1.5 fusion.125
  180.4 1.7 convolution_add_fusion.6
  182.0 1.5 fusion.124
  183.5 1.5 fusion.125
  186.8 1.7 convolution_add_fusion.6
  188.5 1.5 fusion.124
  189.9 1.5 fusion.125
  193.2 1.7 convolution_add_fusion.6
  194.9 3.1 %copy.68 = bf16[8,512,2,128]{3,1,0,2:T(8,128)(2,1)} copy(bf16[8,512,2,128]{3,1,2,0:T(8,128)(2,1)} %get-tuple-element.117) | data formatting | bytes 4194304 | tf_op jit(solution)/shard_map/convert_element_type | solution.py:167
  200.2 0.7 copy.70
  202.0 0.9 copy.69
  202.9 1.0 fusion.44
  203.9 64.0 %reduce-scatter.2.cloned.1.call-done = bf16[256,1,2,128]{3,0,2,1:T(8,128)(2,1)} async-done(((bf16[4096,1,2,128]{3,0,2,1:T(8,128)(2,1)}), bf16[256,1,2,128]{3,0,2,1:T(8,128)(2,1)}) %reduce-scatter.2.cloned.1.call-update) | async-done | bytes 131088 | tf_op jit(solution)/shard_map/reduce_scatter | solution.py:166
  267.9 1.5 slice_bitcast_fusion
  (131 shorter events, 25.6 us)
Async XLA Ops:
  7.2 83.5 %copy-start = (bf16[1,256,1,128]{3,1,2,0:T(8,128)(2,1)S(1)}, bf16[1,256,1,128]{3,1,2,0:T(8,128)(2,1)}, u32[]{:S(2)}) copy-start(bf16[1,256,1,128]{3,1,2,0:T(8,128)(2,1)} %param.18) | copy-start | bytes 196612
  7.2 66.4 %all-gather.3.cloned.1.call-start = ((), (), s32[]{:S(2)}) async-start(), calls=%async_computation.2 | async-start | bytes 1114112 | tf_op jit(solution)/shard_map/all_gather | solution.py:68
  10.7 8.2 %copy-start.10 = (bf16[1,256,1,5,128]{4,1,3,2,0:T(8,128)(2,1)S(1)}, bf16[1,256,1,5,128]{4,1,3,2,0:T(8,128)(2,1)}, u32[]{:S(2)}) copy-start(bf16[1,256,1,5,128]{4,1,3,2,0:T(8,128)(2,1)} %param.16) | copy-start | bytes 983044
  10.7 8.3 %copy-start.12 = (bf16[1,256,1,128]{3,1,2,0:T(8,128)(2,1)S(1)}, bf16[1,256,1,128]{3,1,2,0:T(8,128)(2,1)}, u32[]{:S(2)}) copy-start(bf16[1,256,1,128]{3,1,2,0:T(8,128)(2,1)} %param.17) | copy-start | bytes 196612
  10.7 124.4 %all-to-all-start = ((bf16[8,1,32,5120]{3,2,1,0:T(8,128)(2,1)}), bf16[8,1,32,5120]{3,2,1,0:T(8,128)(2,1)}, u32[]{:S(2)}, u32[]{:S(2)}) async-start(bf16[8,1,32,5120]{3,2,1,0:T(8,128)(2,1)} %stack.10), calls=%async_computation | async-start | bytes 5242880 | tf_op jit(solution)/shard_map/all_to_all | solution.py:62
  16.2 103.4 %all-gather.5.cloned.1.call-start = ((), (), s32[]{:S(2)}) async-start(), calls=%async_computation.3 | async-start | bytes 1114112 | tf_op jit(solution)/shard_map/all_gather | solution.py:69
  17.0 250.9 %reduce-scatter.2.cloned.1.call-start = ((), (), s32[]{:S(2)}) async-start(), calls=%async_computation.4 | async-start | bytes 2228224 | tf_op jit(solution)/shard_map/reduce_scatter | solution.py:166
  17.1 2.9 %copy-start.15 = (f32[64]{0:T(128)}, f32[64]{0:T(128)S(1)}, u32[]{:S(2)}) copy-start(f32[64]{0:T(128)S(1)} %negate_power_fusion) | copy-start | bytes 772
  17.8 2.2 copy-start.13
  19.6 2.2 copy-start.8
  19.9 3.1 %copy-start.1 = (bf16[1,256,1,5,64]{4,1,3,2,0:T(8,128)(2,1)}, bf16[1,256,1,5,64]{4,1,3,2,0:T(8,128)(2,1)S(1)}, u32[]{:S(2)}) copy-start(bf16[1,256,1,5,64]{4,1,3,2,0:T(8,128)(2,1)S(1)} %get-tuple-element.210) | copy-start | bytes 491524
  20.0 3.1 %copy-start.3 = (bf16[1,256,1,5,64]{4,1,3,2,0:T(8,128)(2,1)}, bf16[1,256,1,5,64]{4,1,3,2,0:T(8,128)(2,1)S(1)}, u32[]{:S(2)}) copy-start(bf16[1,256,1,5,64]{4,1,3,2,0:T(8,128)(2,1)S(1)} %get-tuple-element.211) | copy-start | bytes 491524
  141.1 2.5 copy-start.5
  198.0 1.0 copy-start.6
  198.0 1.3 copy-start.2
  198.0 1.4 copy-start.4
  198.0 1.8 copy-start.14
  198.0 1.8 copy-start.16
  199.8 1.5 copy-start.9
  201.0 0.8 copy-start.11
  201.4 1.5 copy-start.7
Sparse Core Ops, SparseCore 0:
  10.5 63.0 all-gather.2
  76.0 43.6 all-gather.4
  198.1 69.7 reduce-scatter.1
